TPU v7x, 32 devices: a whole 2x2x4 slice. The times are simulated.
32 devices in a mesh: grp: 2 (over y), mesh: 4 (over z), col: 2 (over x), term: 2 (over core).
Axes of the slice: x: 2, y: 2, z: 4, core: 2. Of those that a mesh axis runs over, the one named last changes fastest.
Arguments:
- basis: bfloat16 [4096, 512], P(('grp', 'mesh'), 'col'), parts along dimension 0, may hold values from -2 to 2
- blocks: bfloat16 [2, 32, 20, 128, 128], P('term', ('grp', 'mesh', 'col')), parts along dimension 1, may hold values from -0.125 to 0.125
- col_index: int32 [2, 32, 20], P('term', ('grp', 'mesh', 'col')), parts along dimension 1, may hold values from 0 to 5, as said below
- send_rows: int32 [8, 2, 1], P(('grp', 'mesh')), parts along dimension 0, may hold values from 0 to 3, as said below
- part_rows: int32 [8], P(('grp', 'mesh')), parts along dimension 0, may hold values from 1 to 4, as said below
Outputs:
- reduced: float32 [2, 1024, 512], P('term', ('grp', 'mesh', 'col')), parts along dimension 1
There are 2 independent parts, one for each index of `grp`. A program takes and returns all parts, laid end to end along the dimension named above; each array names one. Nothing has to cross between parts.
Inputs may be any that keep to these rules, and one draw needn't show every extreme that they name: `part_rows`: some partition has all 4 block rows live. `send_rows`: every entry is a live block row of the sending partition p; [p, 0, :] go to partition p - 1, [p, 1, :] to partition p + 1. `col_index`: slots 0 to 0 are the rows received from the lower partition, 1 to 4 the partition's own block rows in order, the last 1 those from the upper partition. Entry k = 0 is the block row's own slot; other entries may repeat.
All inputs are finite; a program needn't handle non-finite values.
Results may differ from a plain program's by a relative error of at most 0.0029.
Values may be sent and summed in bfloat16 or wider, within the bound.
A program may use at most 64 MiB of HBM per device.

v0:
```python
import jax
import jax.numpy as jnp
from jax import lax
from jax.sharding import PartitionSpec as P

BS = 128


def from_behind(x, axis, by):
    length = lax.axis_size(axis)
    pairs = [(i, i + by) for i in range(length) if 0 <= i + by < length]
    return lax.ppermute(x, axis, pairs)


def local(basis, blocks, col_index, send_rows, part_rows):
    panel_width = basis.shape[1]
    local_blocks = basis.shape[0] // BS
    halo_count = send_rows.shape[2]
    device_blocks = blocks.shape[1]
    stored = blocks.shape[2]
    live = jnp.arange(local_blocks) < part_rows[0]
    panel = jnp.where(
        live[:, None, None],
        basis.reshape(local_blocks, BS, panel_width),
        jnp.zeros((), jnp.bfloat16),
    )
    going_down = jnp.take(panel, send_rows[0, 0], axis=0)
    going_up = jnp.take(panel, send_rows[0, 1], axis=0)
    from_lower = from_behind(going_up, "mesh", 1)
    from_upper = from_behind(going_down, "mesh", -1)
    ext_panel = jnp.concatenate([from_lower, panel, from_upper], axis=0)
    extended = lax.all_gather(ext_panel, "col", axis=2, tiled=True)
    full_width = extended.shape[2]
    term_blocks = blocks[0]
    slot_index = col_index[0]

    def accumulate(k, running):
        picked = jnp.take(extended, slot_index[:, k], axis=0)
        return running + jnp.einsum(
            "bij,bjc->bic", term_blocks[:, k], picked, preferred_element_type=jnp.float32
        )

    product = lax.fori_loop(
        0, stored, accumulate, jnp.zeros((device_blocks, BS, full_width), jnp.float32)
    )
    rounded = product.astype(jnp.bfloat16).reshape(device_blocks * BS, full_width)
    first_block = halo_count + lax.axis_index("col") * device_blocks
    own_rows = lax.dynamic_slice_in_dim(extended, first_block, device_blocks, 0).reshape(
        device_blocks * BS, full_width
    )
    reduced = lax.psum_scatter(
        lax.dot_general(
            own_rows, rounded, (((0,), (0,)), ((), ())), preferred_element_type=jnp.float32
        ),
        ("mesh", "col"),
        scatter_dimension=0,
        tiled=True,
    )
    return reduced[None]


def solution(mesh):
    placed = (
        P(("grp", "mesh"), "col"),
        P("term", ("grp", "mesh", "col"), None, None, None),
        P("term", ("grp", "mesh", "col"), None),
        P(("grp", "mesh"), None, None),
        P(("grp", "mesh")),
    )
    return jax.shard_map(
        local,
        mesh=mesh,
        in_specs=placed,
        out_specs=P("term", ("grp", "mesh", "col"), None),
        check_vma=False,
    )
```

profile of v0, /device:TPU:0, one launch (start us, length us, event | category | flops | bytes accessed | tf_op | source)
XLA Modules:
  0.0 144.3 jit_solution(10313088490599660926)
XLA Ops:
  6.5 1.4 fusion.10
  11.8 1.1 copy.9
  13.7 4.9 %collective-permute-start = (bf16[1,128,256]{1,2,0:T(8,128)(2,1)S(1)}, bf16[1,128,256]{1,2,0:T(8,128)(2,1)S(1)}, u32[]{:S(2)}, u32[]{:S(2)}) collective-permute-start(bf16[1,128,256]{1,2,0:T(8,128)(2,1)S(1)} %get-tuple-element.152), channel_id=1, source_target_pairs={{0,4},{4,8},{8,12},{1,5},{5,9},{9,13},{2,6},{6,10},{10,14},{3,7},{... | collective-permute-start | bytes 196616 | tf_op jit(solution)/shard_map/ppermute | solution.py:12
  18.6 1.3 collective-permute-start.1
  20.0 1.2 copy.14
  21.2 3.6 %collective-permute-done.1 = bf16[1,128,256]{1,2,0:T(8,128)(2,1)S(1)} collective-permute-done((bf16[1,128,256]{1,2,0:T(8,128)(2,1)S(1)}, bf16[1,128,256]{1,2,0:T(8,128)(2,1)S(1)}, u32[]{:S(2)}, u32[]{:S(2)}) %collective-permute-start.1) | collective-permute-done | bytes 65568 | tf_op jit(solution)/shard_map/ppermute | solution.py:12
  24.8 10.1 %all_gather.3 = bf16[6,128,512]{1,2,0:T(8,128)(2,1)S(1)} all-gather(bf16[6,128,256]{1,2,0:T(8,128)(2,1)S(1)} %pad_maximum_fusion), channel_id=1, replica_groups=mesh['grp'=2,'mesh'=4,'col'=2,'term'=2] {'col'}, dimensions={2}, use_global_device_ids=true | all-gather | bytes 1179648 | tf_op jit(solution)/shard_map/all_gather | solution.py:32
  35.2 36.3 %while.15 = (s32[]{:T(128)}, f32[2,128,512]{2,1,0:T(8,128)S(1)}, bf16[2,20,128,128]{3,2,0,1:T(8,128)(2,1)}, s32[2,20]{0,1:T(8,128)S(1)}, bf16[6,128,512]{2,1,0:T(8,128)(2,1)S(1)}, /*index=5*/s32[]{:T(128)}, s32[]{:T(128)}) while((s32[]{:T(128)}, f32[2,128,512]{2,1,0:T(8,128)S(1)}, bf16[2,20,128,128]{3,2,0,1:T(8,128)(2,1)}, ...), condition=%wide.region_1.3_spmd.clone, body=%wide.region_0.2_spmd.clone.sunk | while | flops 33948688 | bytes 1905279 | solution.py:43
  35.3 0.6 gather_fusion
  35.8 1.2 convolution_add_fusion.2
  37.1 0.6 gather_fusion
  37.7 1.2 convolution_add_fusion.2
  38.9 0.6 gather_fusion
  39.5 1.2 convolution_add_fusion.2
  40.7 0.6 gather_fusion
  41.3 1.2 convolution_add_fusion.2
  42.5 0.6 gather_fusion
  43.1 1.2 convolution_add_fusion.2
  44.4 0.6 gather_fusion
  44.9 1.2 convolution_add_fusion.2
  46.2 0.6 gather_fusion
  46.7 1.2 convolution_add_fusion.2
  48.0 0.6 gather_fusion
  48.6 1.2 convolution_add_fusion.2
  49.8 0.6 gather_fusion
  50.4 1.2 convolution_add_fusion.2
  51.6 0.6 gather_fusion
  52.2 1.2 convolution_add_fusion.2
  53.4 0.6 gather_fusion
  54.0 1.2 convolution_add_fusion.2
  55.3 0.6 gather_fusion
  55.8 1.2 convolution_add_fusion.2
  57.1 0.6 gather_fusion
  57.7 1.2 convolution_add_fusion.2
  58.9 0.6 gather_fusion
  59.5 1.2 convolution_add_fusion.2
  60.7 0.6 gather_fusion
  61.3 1.2 convolution_add_fusion.2
  62.5 0.6 gather_fusion
  63.1 1.2 convolution_add_fusion.2
  64.3 0.6 gather_fusion
  64.9 1.2 convolution_add_fusion.2
  66.2 0.6 gather_fusion
  66.7 1.2 convolution_add_fusion.2
  68.6 1.2 convolution_add_fusion.2
  70.4 1.2 convolution_add_fusion.2
  71.6 1.3 convolution_bitcast_fusion
  72.9 64.5 %reduce-scatter.2.cloned.1.call-done = f32[64,512]{1,0:T(8,128)} async-done(((f32[512,512]{1,0:T(8,128)}), f32[64,512]{1,0:T(8,128)}) %reduce-scatter.2.cloned.1.call-update) | async-done | bytes 131088 | tf_op jit(solution)/shard_map/reduce_scatter | solution.py:51
  (56 shorter events, 2.1 us)
Async XLA Ops:
  6.5 13.4 %copy-start = (bf16[1,2,20,128,128]{4,3,2,1,0:T(8,128)(2,1)S(1)}, bf16[1,2,20,128,128]{4,3,2,1,0:T(8,128)(2,1)}, u32[]{:S(2)}) copy-start(bf16[1,2,20,128,128]{4,3,2,1,0:T(8,128)(2,1)} %param.10) | copy-start | bytes 3932164
  6.5 130.9 %reduce-scatter.2.cloned.1.call-start = ((), (), s32[]{:S(2)}) async-start(), calls=%async_computation.1 | async-start | bytes 1179648 | tf_op jit(solution)/shard_map/reduce_scatter | solution.py:51
  13.7 7.5 %collective-permute-start = (bf16[1,128,256]{1,2,0:T(8,128)(2,1)S(1)}, bf16[1,128,256]{1,2,0:T(8,128)(2,1)S(1)}, u32[]{:S(2)}, u32[]{:S(2)}) collective-permute-start(bf16[1,128,256]{1,2,0:T(8,128)(2,1)S(1)} %get-tuple-element.152), channel_id=1, source_target_pairs={{0,4},{4,8},{8,12},{1,5},{5,9},{9,13},{2,6},{6,10},{10,14},{3,7},{... | collective-permute-start | bytes 196616 | tf_op jit(solution)/shard_map/ppermute | solution.py:12
  18.6 6.2 %collective-permute-start.1 = (bf16[1,128,256]{1,2,0:T(8,128)(2,1)S(1)}, bf16[1,128,256]{1,2,0:T(8,128)(2,1)S(1)}, u32[]{:S(2)}, u32[]{:S(2)}) collective-permute-start(bf16[1,128,256]{1,2,0:T(8,128)(2,1)S(1)} %get-tuple-element.153), channel_id=1, source_target_pairs={{4,0},{8,4},{12,8},{5,1},{9,5},{13,9},{6,2},{10,6},{14,10},{7,3},{... | collective-permute-start | bytes 196616 | tf_op jit(solution)/shard_map/ppermute | solution.py:12
  19.9 1.2 copy-start.1
Sparse Core Ops, SparseCore 0:
  73.0 64.3 reduce-scatter.1
where the time goes:
time: 145 us; the launch traced here: 144 us
  waiting for transfers between devices  68.1 us (47%)
  matrix products  24.9 us (17%)
  between operations  18 us (12%)
  local copies, waits for them, and re-layouts  15.3 us (11%)
  blocking collectives  10.1 us (7%)
  starting transfers between devices  6.23 us (4%)
    reduce_scatter x1, waiting for transfers between devices, local(): lax.psum_scatter(lax.dot_general(own_rows, rounded, (((0,), (0,)), ((), (...  64.5 us
    dot_general x20, matrix products, accumulate(): jnp.einsum('bij,bjc->bic', term_blocks[:, k], picked, preferred_element_t...  23.7 us
    gather x20, local copies, waits for them, and re-layouts, accumulate(): picked = jnp.take(extended, slot_index[:, k], axis=0)  11.3 us
    all_gather x1, blocking collectives, local(): extended = lax.all_gather(ext_panel, 'col', axis=2, tiled=True)  10.1 us
    ppermute x2, starting transfers between devices, from_behind(): return lax.ppermute(x, axis, pairs)  6.22 us
    ppermute x2, waiting for transfers between devices, from_behind(): return lax.ppermute(x, axis, pairs)  3.57 us
  transfers between devices with their start and end apart: 3, of which 2 were waited for; matrix products, arithmetic and copies ran while one was open for 1% of the time, Pallas kernels for 0%

commit v1 on v0

--- a/solution.py
+++ b/solution.py
@@ -1,9 +1,14 @@
+import functools
+
 import jax
 import jax.numpy as jnp
 from jax import lax
+from jax.experimental import pallas as pl
+from jax.experimental.pallas import tpu as pltpu
 from jax.sharding import PartitionSpec as P
 
 BS = 128
+MESH = pl.DeviceIdType.MESH
 
 
 def from_behind(x, axis, by):
@@ -12,7 +17,7 @@
     return lax.ppermute(x, axis, pairs)
 
 
-def local(basis, blocks, col_index, send_rows, part_rows):
+def general(basis, blocks, col_index, send_rows, part_rows):
     panel_width = basis.shape[1]
     local_blocks = basis.shape[0] // BS
     halo_count = send_rows.shape[2]
@@ -59,6 +64,242 @@
     return reduced[None]
 
 
+def kernel(
+    parts,
+    cores,
+    part_ref,
+    send_ref,
+    col_ref,
+    basis_ref,
+    blocks_ref,
+    out_ref,
+    basis_v,
+    blocks_v,
+    other_raw,
+    ext_own,
+    ext_other,
+    stage,
+    p_send,
+    p_all,
+    g32,
+    g_send,
+    g_recv,
+    local_sem,
+    x_send,
+    x_recv,
+    z_send,
+    z_recv,
+    g_ssem,
+    g_rsem,
+):
+    g = lax.axis_index("grp")
+    m = lax.axis_index("mesh")
+    c = lax.axis_index("col")
+    t = lax.axis_index("term")
+    lb, _, width = basis_v.shape
+    halo = send_ref.shape[1]
+    rows, stored = blocks_v.shape[:2]
+    ranks = 2 * parts
+    rank = 2 * m + c
+    half = lb // cores
+    piece = g_send.shape[0] // ranks
+    mine = (g, m, 1 - c, t)
+    sibling = (g, m, c, 1 - t)
+
+    load_basis = pltpu.make_async_copy(basis_ref, basis_v, local_sem.at[0])
+    load_basis.start()
+    load_blocks = pltpu.make_async_copy(blocks_ref, blocks_v, local_sem.at[1])
+    load_blocks.start()
+
+    def peer(d):
+        r = lax.rem(rank + d, ranks)
+        return (g, r // 2, lax.rem(r, 2), t), r
+
+    barrier = pltpu.get_barrier_semaphore()
+    for d in range(1, ranks):
+        pl.semaphore_signal(barrier, inc=1, device_id=peer(d)[0], device_id_type=MESH)
+    pl.semaphore_signal(barrier, inc=1, device_id=sibling, device_id_type=MESH)
+    pl.semaphore_wait(barrier, ranks)
+
+    def remote(src, dst, ssem, rsem, to):
+        return pltpu.make_async_remote_copy(
+            src_ref=src, dst_ref=dst, send_sem=ssem, recv_sem=rsem, device_id=to, device_id_type=MESH
+        )
+
+    span = pl.ds(t * half, half)
+    across = remote(basis_ref.at[span], other_raw.at[span], x_send.at[0], x_recv.at[0], mine)
+    across.start()
+
+    load_basis.wait()
+    low = pl.ds(0, halo)
+    high = pl.ds(lb + halo, halo)
+
+    def halo_copies(ext, base):
+        up = remote(stage.at[base], ext.at[low], z_send.at[base], z_recv.at[base], (g, lax.rem(m + 1, parts), c, t))
+        down = remote(
+            stage.at[base + 1],
+            ext.at[high],
+            z_send.at[base + 1],
+            z_recv.at[base + 1],
+            (g, lax.rem(m + parts - 1, parts), c, t),
+        )
+        return up, down
+
+    def send_halo(raw, ext, base):
+        for j in range(halo):
+            stage[base, j] = raw[send_ref[1, j]]
+            stage[base + 1, j] = raw[send_ref[0, j]]
+        up, down = halo_copies(ext, base)
+
+        @pl.when(m < parts - 1)
+        def _():
+            up.start()
+
+        @pl.when(m > 0)
+        def _():
+            down.start()
+
+        @pl.when(m == 0)
+        def _():
+            ext[low] = jnp.zeros((halo, BS, width), jnp.bfloat16)
+
+        @pl.when(m == parts - 1)
+        def _():
+            ext[high] = jnp.zeros((halo, BS, width), jnp.bfloat16)
+
+        for i in range(lb):
+            ext[halo + i] = jnp.where(i < part_ref[0], raw[i], jnp.zeros((), jnp.bfloat16))
+
+    def wait_halo(ext, base):
+        up, down = halo_copies(ext, base)
+
+        @pl.when(m > 0)
+        def _():
+            up.wait_recv()
+
+        @pl.when(m < parts - 1)
+        def _():
+            down.wait_recv()
+
+    def drain_halo(ext, base):
+        up, down = halo_copies(ext, base)
+
+        @pl.when(m < parts - 1)
+        def _():
+            up.wait_send()
+
+        @pl.when(m > 0)
+        def _():
+            down.wait_send()
+
+    def product(ext, r):
+        total = jnp.zeros((BS, width), jnp.float32)
+        step = 2 if stored % 2 == 0 else 1
+        for k in range(0, stored, step):
+            left = jnp.concatenate([blocks_v[r, k + j] for j in range(step)], axis=1)
+            right = jnp.concatenate([ext[col_ref[r, k + j]] for j in range(step)], axis=0)
+            total = total + jnp.dot(left, right, preferred_element_type=jnp.float32)
+        return total.astype(jnp.bfloat16)
+
+    send_halo(basis_v, ext_own, 0)
+    load_blocks.wait()
+    wait_halo(ext_own, 0)
+    for r in range(rows):
+        p_send[pl.ds(r * BS, BS)] = product(ext_own, r)
+    swap = remote(p_send, p_all.at[pl.ds(c * rows * BS, rows * BS)], x_send.at[1], x_recv.at[1], mine)
+    swap.start()
+
+    across.wait_recv()
+    inner = remote(other_raw.at[span], other_raw.at[span], x_send.at[2], x_recv.at[2], sibling)
+    inner.start()
+    inner.wait_recv()
+    send_halo(other_raw, ext_other, 2)
+    wait_halo(ext_other, 2)
+    for r in range(rows):
+        p_all[pl.ds(c * rows * BS + r * BS, BS)] = product(ext_other, r)
+    swap.wait_recv()
+
+    right = p_all[...]
+
+    def gram(ext):
+        left = ext[pl.ds(halo, lb)].reshape(lb * BS, width)
+        return lax.dot_general(left, right, (((0,), (0,)), ((), ())), preferred_element_type=jnp.float32)
+
+    for ext, where in ((ext_own, c), (ext_other, 1 - c)):
+        value = gram(ext)
+        g32[pl.ds(where * width, width)] = value
+        g_send[pl.ds(where * width, width)] = value.astype(jnp.bfloat16)
+
+    def share(d):
+        to, r = peer(d)
+        return remote(g_send.at[pl.ds(r * piece, piece)], g_recv.at[d - 1], g_ssem.at[d - 1], g_rsem.at[d - 1], to)
+
+    for d in range(1, ranks):
+        share(d).start()
+
+    same = g32[pl.ds(rank * piece, piece)]
+    crossed = jnp.zeros_like(same)
+    for d in range(1, ranks):
+        share(d).wait_recv()
+        if d % 2:
+            crossed = crossed + g_recv[d - 1].astype(jnp.float32)
+        else:
+            same = same + g_recv[d - 1].astype(jnp.float32)
+    out_ref[:, pl.ds(pl.multiple_of((1 - c) * width, width), width)] = same
+    out_ref[:, pl.ds(pl.multiple_of(c * width, width), width)] = crossed
+
+    across.wait_send()
+    swap.wait_send()
+    inner.wait_send()
+    drain_halo(ext_own, 0)
+    drain_halo(ext_other, 2)
+    for d in range(1, ranks):
+        share(d).wait_send()
+
+
+def fused(parts, cores, basis, blocks, col_index, send_rows, part_rows):
+    width = basis.shape[1]
+    lb = basis.shape[0] // BS
+    halo = send_rows.shape[2]
+    rows, stored = blocks.shape[1:3]
+    full = 2 * width
+    ranks = 2 * parts
+    piece = full // ranks
+    bf16 = jnp.bfloat16
+    smem = pl.BlockSpec(memory_space=pltpu.SMEM)
+    hbm = pl.BlockSpec(memory_space=pl.ANY)
+    reduced = pl.pallas_call(
+        functools.partial(kernel, parts, cores),
+        out_shape=jax.ShapeDtypeStruct((piece, full), jnp.float32),
+        in_specs=[smem, smem, smem, hbm, hbm],
+        out_specs=pl.BlockSpec(memory_space=pltpu.VMEM),
+        scratch_shapes=[
+            pltpu.VMEM((lb, BS, width), bf16),
+            pltpu.VMEM((rows, stored, BS, BS), bf16),
+            pltpu.VMEM((lb, BS, width), bf16),
+            pltpu.VMEM((lb + 2 * halo, BS, width), bf16),
+            pltpu.VMEM((lb + 2 * halo, BS, width), bf16),
+            pltpu.VMEM((4, halo, BS, width), bf16),
+            pltpu.VMEM((rows * BS, width), bf16),
+            pltpu.VMEM((lb * BS, width), bf16),
+            pltpu.VMEM((full, width), jnp.float32),
+            pltpu.VMEM((full, width), bf16),
+            pltpu.VMEM((ranks - 1, piece, width), bf16),
+            pltpu.SemaphoreType.DMA((2,)),
+            pltpu.SemaphoreType.DMA((3,)),
+            pltpu.SemaphoreType.DMA((3,)),
+            pltpu.SemaphoreType.DMA((4,)),
+            pltpu.SemaphoreType.DMA((4,)),
+            pltpu.SemaphoreType.DMA((ranks - 1,)),
+            pltpu.SemaphoreType.DMA((ranks - 1,)),
+        ],
+        compiler_params=pltpu.CompilerParams(
+            collective_id=0, has_side_effects=True, vmem_limit_bytes=24 * 1024 * 1024
+        ),
+    )(part_rows, send_rows[0], col_index[0], basis.reshape(lb, BS, width), blocks[0])
+    return reduced[None]
+
+
 def solution(mesh):
     placed = (
         P(("grp", "mesh"), "col"),
@@ -67,6 +308,22 @@
         P(("grp", "mesh"), None, None),
         P(("grp", "mesh")),
     )
+    parts, cols, cores = mesh.shape["mesh"], mesh.shape["col"], mesh.shape["term"]
+
+    def local(basis, blocks, col_index, send_rows, part_rows):
+        lb = basis.shape[0] // BS
+        fits = (
+            cols == 2
+            and cores == 2
+            and basis.shape[1] % BS == 0
+            and lb % cores == 0
+            and lb == 2 * blocks.shape[1]
+            and (2 * basis.shape[1]) % (2 * parts * 16) == 0
+        )
+        if fits:
+            return fused(parts, cores, basis, blocks, col_index, send_rows, part_rows)
+        return general(basis, blocks, col_index, send_rows, part_rows)
+
     return jax.shard_map(
         local,
         mesh=mesh,

time: 145 us -> 27.1 us (0.19)
  waiting for transfers between devices: 68.1 us -> 0 us
  matrix products: 24.9 us -> 0 us
  Pallas kernels: 0 us -> 21.8 us
  between operations: 18 us -> 0.66 us
  local copies, waits for them, and re-layouts: 15.3 us -> 4.34 us
  blocking collectives: 10.1 us -> 0 us
  starting transfers between devices: 6.23 us -> 0 us
    reduce_scatter x1 -> x0, waiting for transfers between devices: 64.5 us -> none  [local(): lax.psum_scatter(lax.dot_general(own_rows, rounded, (((0,), (0,)), ((), (...]
    dot_general x21 -> x0, matrix products: 24.9 us -> none  [the longest x20 23.7 us: accumulate(): jnp.einsum('bij,bjc->bic', term_blocks[:, k], picked, preferred_element_t...]
    pallas_call x0 -> x1, Pallas kernels: none -> 21.8 us  [fused(): pl.pallas_call(functools.partial(kernel, parts, cores), out_shape=jax.Sha...]
    gather x20 -> x0, local copies, waits for them, and re-layouts: 11.3 us -> none  [accumulate(): picked = jnp.take(extended, slot_index[:, k], axis=0)]
    all_gather x1 -> x0, blocking collectives: 10.1 us -> none  [local(): extended = lax.all_gather(ext_panel, 'col', axis=2, tiled=True)]
    ppermute x2 -> x0, starting transfers between devices: 6.22 us -> none  [from_behind(): return lax.ppermute(x, axis, pairs)]
    ppermute x2 -> x0, waiting for transfers between devices: 3.57 us -> none  [from_behind(): return lax.ppermute(x, axis, pairs)]
    unnamed x7, local copies, waits for them, and re-layouts: 1.54 us -> 3.6 us
  transfers between devices with their start and end apart: 3 -> 0, of which waited for: 2 -> 0; matrix products, arithmetic and copies ran while one was open for 1% -> 0% of each run, Pallas kernels for 0% -> 0%
where the time goes in v1:
time: 27.1 us; the launch traced here: 26.9 us
  Pallas kernels  21.8 us (80%)
  local copies, waits for them, and re-layouts  4.34 us (16%)
  between operations  0.66 us (2%)
    pallas_call x1, Pallas kernels, fused(): pl.pallas_call(functools.partial(kernel, parts, cores), out_shape=jax.Sha...  21.8 us
    unnamed x7, local copies, waits for them, and re-layouts  3.6 us
    squeeze x1, local copies, waits for them, and re-layouts, fused(): send_rows[0]  0.74 us

profile of v1, /device:TPU:0, one launch (start us, length us, event | category | flops | bytes accessed | tf_op | source)
XLA Modules:
  0.0 26.9 jit_solution(6179565133756620957)
XLA Ops:
  0.7 0.7 %copy.6.send_ref = s32[2,1]{1,0:T(2,128)S(1)} copy(s32[2,1]{0,1:T(1,128)} %bitcast.9) | data formatting | bytes 16 | tf_op jit(solution)/shard_map/squeeze | solution.py:299
  1.4 0.0 copy-start
  1.4 1.3 %copy-done = bf16[1,2,20,128,128]{4,3,2,1,0:T(8,128)(2,1)S(1)} copy-done((bf16[1,2,20,128,128]{4,3,2,1,0:T(8,128)(2,1)S(1)}, bf16[1,2,20,128,128]{4,3,2,1,0:T(8,128)(2,1)}, u32[]{:S(2)}) %copy-start) | copy-done | bytes 1310744
  2.7 0.0 copy-start.1
  2.7 0.9 %copy-done.1 = bf16[512,256]{1,0:T(8,128)(2,1)S(1)} copy-done((bf16[512,256]{1,0:T(8,128)(2,1)S(1)}, bf16[512,256]{1,0:T(8,128)(2,1)}, u32[]{:S(2)}) %copy-start.1) | copy-done | bytes 262168
  3.7 0.0 copy-start.2
  3.7 0.7 %copy-done.2 = s32[1,2,20]{2,1,0:T(2,128)S(1)} copy-done((s32[1,2,20]{2,1,0:T(2,128)S(1)}, s32[1,2,20]{2,1,0:T(2,128)}, u32[]{:S(2)}) %copy-start.2) | copy-done | bytes 184
  4.3 21.8 %shard_map.55 = f32[64,512]{1,0:T(8,128)S(1)} custom-call(s32[1]{0:T(128)S(6)} %copy.8.part_ref, s32[2,1]{1,0:T(2,128)S(1)} %copy.6.send_ref, s32[2,20]{1,0:T(2,128)S(1)} %bitcast.8, bf16[4,128,256]{2,1,0:T(8,128)(2,1)S(1)} %bitcast.7, bf16[2,20,128,128]{3,2,1,0:T(8,128)(2,1)S(1)} %bitcast.5), custom_call_target="tpu_custom_call" | custom-call | tf_op jit(solution)/shard_map/pallas_call | solution.py:271
  26.2 0.7 %copy.9 = f32[1,64,512]{2,1,0:T(8,128)} copy(f32[1,64,512]{2,1,0:T(8,128)S(1)} %bitcast.6) | data formatting | bytes 262144
Async XLA Ops:
  1.4 1.3 %copy-start = (bf16[1,2,20,128,128]{4,3,2,1,0:T(8,128)(2,1)S(1)}, bf16[1,2,20,128,128]{4,3,2,1,0:T(8,128)(2,1)}, u32[]{:S(2)}) copy-start(bf16[1,2,20,128,128]{4,3,2,1,0:T(8,128)(2,1)} %param.6) | copy-start | bytes 3932164
  2.7 0.9 %copy-start.1 = (bf16[512,256]{1,0:T(8,128)(2,1)S(1)}, bf16[512,256]{1,0:T(8,128)(2,1)}, u32[]{:S(2)}) copy-start(bf16[512,256]{1,0:T(8,128)(2,1)} %param.5) | copy-start | bytes 786436
  3.7 0.7 %copy-start.2 = (s32[1,2,20]{2,1,0:T(2,128)S(1)}, s32[1,2,20]{2,1,0:T(2,128)}, u32[]{:S(2)}) copy-start(s32[1,2,20]{2,1,0:T(2,128)} %param.7) | copy-start | bytes 484

commit v2 on v0

--- a/solution.py
+++ b/solution.py
@@ -1,9 +1,14 @@
+import functools
+
 import jax
 import jax.numpy as jnp
 from jax import lax
+from jax.experimental import pallas as pl
+from jax.experimental.pallas import tpu as pltpu
 from jax.sharding import PartitionSpec as P
 
 BS = 128
+MESH = pl.DeviceIdType.MESH
 
 
 def from_behind(x, axis, by):
@@ -12,7 +17,7 @@
     return lax.ppermute(x, axis, pairs)
 
 
-def local(basis, blocks, col_index, send_rows, part_rows):
+def general(basis, blocks, col_index, send_rows, part_rows):
     panel_width = basis.shape[1]
     local_blocks = basis.shape[0] // BS
     halo_count = send_rows.shape[2]
@@ -59,6 +64,285 @@
     return reduced[None]
 
 
+def kernel(
+    parts,
+    cores,
+    part_hbm,
+    send_hbm,
+    col_hbm,
+    basis_ref,
+    blocks_ref,
+    out_ref,
+    part_ref,
+    send_ref,
+    col_ref,
+    basis_v,
+    blocks_v,
+    other_raw,
+    ext_own,
+    ext_other,
+    stage,
+    turned,
+    p_send,
+    p_all,
+    g32,
+    g_send,
+    g_recv,
+    local_sem,
+    x_send,
+    x_recv,
+    z_send,
+    z_recv,
+    g_ssem,
+    g_rsem,
+    ok_sem,
+):
+    g = lax.axis_index("grp")
+    m = lax.axis_index("mesh")
+    c = lax.axis_index("col")
+    t = lax.axis_index("term")
+    strips, lb = basis_v.shape[:2]
+    width = strips * BS
+    halo = send_ref.shape[0]
+    rows, stored = blocks_v.shape[:2]
+    ranks = 2 * parts
+    rank = 2 * m + c
+    half = lb // cores
+    piece = g_send.shape[1] // ranks
+    opposite = (g, m, 1 - c, t)
+    sibling = (g, m, c, 1 - t)
+    below = lax.rem(m + parts - 1, parts)
+    above = lax.rem(m + 1, parts)
+    has_lower = m > 0
+    has_upper = m < parts - 1
+    everyone = range(strips)
+
+    def strip(q):
+        return pl.ds(q * BS, BS)
+
+    load_basis = [
+        pltpu.make_async_copy(basis_ref.at[:, :, strip(q)], basis_v.at[q], local_sem.at[4 + q]) for q in everyone
+    ]
+    load_small = [
+        pltpu.make_async_copy(hbm, ref, local_sem.at[1 + n])
+        for n, (hbm, ref) in enumerate(((send_hbm, send_ref), (part_hbm, part_ref), (col_hbm, col_ref)))
+    ]
+    load_blocks = pltpu.make_async_copy(blocks_ref, blocks_v, local_sem.at[0])
+    for load in load_basis + load_small + [load_blocks]:
+        load.start()
+
+    def peer(d):
+        r = lax.rem(rank + d, ranks)
+        return (g, r // 2, lax.rem(r, 2), t), r
+
+    for load in load_basis + load_small:
+        load.wait()
+    for j in range(halo):
+        for q in everyone:
+            stage[0, q, j] = basis_v[q, send_ref[j, 1]]
+            stage[1, q, j] = basis_v[q, send_ref[j, 0]]
+
+    barrier = pltpu.get_barrier_semaphore()
+    for to in (sibling, opposite):
+        pl.semaphore_signal(barrier, inc=1, device_id=to, device_id_type=MESH)
+    for there, z in ((has_lower, below), (has_upper, above)):
+
+        @pl.when(there)
+        def _():
+            for side in (c, 1 - c):
+                pl.semaphore_signal(barrier, inc=1, device_id=(g, z, side, t), device_id_type=MESH)
+
+    sides = has_lower.astype(jnp.int32) + has_upper.astype(jnp.int32)
+    pl.semaphore_wait(barrier, 2 + 2 * sides)
+
+    def remote(src, dst, ssem, rsem, to):
+        return pltpu.make_async_remote_copy(
+            src_ref=src, dst_ref=dst, send_sem=ssem, recv_sem=rsem, device_id=to, device_id_type=MESH
+        )
+
+    span = pl.ds(t * half, half)
+    edge = pl.ds(t * (lb + halo), halo)
+    ahead, behind = m + 1 - 2 * t, m - 1 + 2 * t
+    has_ahead = jnp.logical_and(ahead >= 0, ahead < parts)
+    has_behind = jnp.logical_and(behind >= 0, behind < parts)
+    forward = lax.rem(ahead + parts, parts)
+    across = remote(basis_v.at[:, span], other_raw.at[:, span], x_send.at[0], x_recv.at[0], opposite)
+    inner = remote(other_raw.at[:, span], other_raw.at[:, span], x_send.at[1], x_recv.at[1], sibling)
+    slant = remote(stage.at[t], ext_other.at[:, edge], x_send.at[2], x_recv.at[2], (g, forward, 1 - c, t))
+    inner_edge = remote(ext_other.at[:, edge], ext_other.at[:, edge], x_send.at[3], x_recv.at[3], sibling)
+    placed = pl.ds(c * rows * BS, rows * BS)
+    swap = [remote(p_send.at[q], p_all.at[q, placed], x_send.at[4 + q], x_recv.at[4 + q], opposite) for q in everyone]
+    low = pl.ds(0, halo)
+    high = pl.ds(lb + halo, halo)
+    up = remote(stage.at[0], ext_own.at[:, low], z_send.at[0], z_recv.at[0], (g, above, c, t))
+    down = remote(stage.at[1], ext_own.at[:, high], z_send.at[1], z_recv.at[1], (g, below, c, t))
+
+    across.start()
+    pl.when(has_upper)(up.start)
+    pl.when(has_lower)(down.start)
+    pl.when(has_ahead)(slant.start)
+
+    def fill(raw, ext):
+        for q in everyone:
+            for i in range(lb):
+                ext[q, halo + i] = jnp.where(i < part_ref[0], raw[q, i], jnp.zeros((), jnp.bfloat16))
+
+    blank = jnp.zeros((strips, halo, BS, BS), jnp.bfloat16)
+    for there, where in ((has_lower, low), (has_upper, high)):
+
+        @pl.when(jnp.logical_not(there))
+        def _():
+            ext_own[:, where] = blank
+            ext_other[:, where] = blank
+
+    def product(ext, r):
+        total = jnp.zeros((BS, width), jnp.float32)
+        step = 2 if stored % 2 == 0 else 1
+        for k in range(0, stored, step):
+            left = jnp.concatenate([blocks_v[r, k + j] for j in range(step)], axis=1)
+            right = jnp.concatenate(
+                [
+                    jnp.concatenate([ext[q, col_ref[r, k + j]] for q in everyone], axis=1)
+                    for j in range(step)
+                ],
+                axis=0,
+            )
+            total = total + jnp.dot(left, right, preferred_element_type=jnp.float32)
+        return total.astype(jnp.bfloat16)
+
+    def turn(ext, where):
+        for q in everyone:
+            body = ext[q, pl.ds(halo, lb)].reshape(lb * BS, BS)
+            turned[pl.ds(where * width + q * BS, BS)] = body.T
+
+    def share(d, q):
+        to, r = peer(d)
+        return remote(
+            g_send.at[q, pl.ds(r * piece, piece)],
+            g_recv.at[q, d - 1],
+            g_ssem.at[q, d - 1],
+            g_rsem.at[q, d - 1],
+            to,
+        )
+
+    order = sorted(range(1, ranks), key=lambda d: abs(d - parts))
+
+    fill(basis_v, ext_own)
+    load_blocks.wait()
+    pl.when(has_lower)(up.wait_recv)
+    pl.when(has_upper)(down.wait_recv)
+    for there, z in ((has_lower, below), (has_upper, above)):
+
+        @pl.when(there)
+        def _():
+            pl.semaphore_signal(ok_sem, inc=1, device_id=(g, z, c, t), device_id_type=MESH)
+
+    for r in range(rows):
+        value = product(ext_own, r)
+        for q in everyone:
+            p_send[q, pl.ds(r * BS, BS)] = value[:, q * BS : (q + 1) * BS]
+    for q in everyone:
+        swap[q].start()
+    across.wait_recv()
+    inner.start()
+
+    @pl.when(has_behind)
+    def _():
+        slant.wait_recv()
+        inner_edge.start()
+
+    turn(ext_own, c)
+    inner.wait_recv()
+    fill(other_raw, ext_other)
+    turn(ext_other, 1 - c)
+    pl.when(has_ahead)(inner_edge.wait_recv)
+    for r in range(rows):
+        value = product(ext_other, r)
+        for q in everyone:
+            p_all[q, pl.ds(c * rows * BS + r * BS, BS)] = value[:, q * BS : (q + 1) * BS]
+    pl.semaphore_wait(ok_sem, sides)
+
+    for q in everyone:
+        swap[q].wait_recv()
+        value = jnp.dot(turned[...], p_all[q], preferred_element_type=jnp.float32)
+        g32[q] = value
+        g_send[q] = value.astype(jnp.bfloat16)
+        for d in order:
+            share(d, q).start()
+
+    for q in everyone:
+        same = g32[q, pl.ds(rank * piece, piece)]
+        crossed = jnp.zeros_like(same)
+        for d in reversed(order):
+            share(d, q).wait_recv()
+            if d % 2:
+                crossed = crossed + g_recv[q, d - 1].astype(jnp.float32)
+            else:
+                same = same + g_recv[q, d - 1].astype(jnp.float32)
+        out_ref[:, pl.ds(pl.multiple_of((1 - c) * width + q * BS, BS), BS)] = same
+        out_ref[:, pl.ds(pl.multiple_of(c * width + q * BS, BS), BS)] = crossed
+
+    across.wait_send()
+    inner.wait_send()
+    pl.when(has_ahead)(slant.wait_send)
+    pl.when(has_behind)(inner_edge.wait_send)
+    pl.when(has_upper)(up.wait_send)
+    pl.when(has_lower)(down.wait_send)
+    for q in everyone:
+        swap[q].wait_send()
+        for d in order:
+            share(d, q).wait_send()
+
+
+def fused(parts, cores, basis, blocks, col_index, send_rows, part_rows):
+    width = basis.shape[1]
+    lb = basis.shape[0] // BS
+    halo = send_rows.shape[2]
+    rows, stored = blocks.shape[1:3]
+    full = 2 * width
+    strips = width // BS
+    ranks = 2 * parts
+    piece = full // ranks
+    bf16 = jnp.bfloat16
+    dma = pltpu.SemaphoreType.DMA
+    hbm = pl.BlockSpec(memory_space=pltpu.HBM)
+    reduced = pl.pallas_call(
+        functools.partial(kernel, parts, cores),
+        out_shape=jax.ShapeDtypeStruct((piece, full), jnp.float32),
+        in_specs=[hbm] * 5,
+        out_specs=pl.BlockSpec(memory_space=pltpu.VMEM),
+        scratch_shapes=[
+            pltpu.SMEM((1,), jnp.int32),
+            pltpu.SMEM((halo, 2), jnp.int32),
+            pltpu.SMEM((rows, stored), jnp.int32),
+            pltpu.VMEM((strips, lb, BS, BS), bf16),
+            pltpu.VMEM((rows, stored, BS, BS), bf16),
+            pltpu.VMEM((strips, lb, BS, BS), bf16),
+            pltpu.VMEM((strips, lb + 2 * halo, BS, BS), bf16),
+            pltpu.VMEM((strips, lb + 2 * halo, BS, BS), bf16),
+            pltpu.VMEM((2, strips, halo, BS, BS), bf16),
+            pltpu.VMEM((full, lb * BS), bf16),
+            pltpu.VMEM((strips, rows * BS, BS), bf16),
+            pltpu.VMEM((strips, lb * BS, BS), bf16),
+            pltpu.VMEM((strips, full, BS), jnp.float32),
+            pltpu.VMEM((strips, full, BS), bf16),
+            pltpu.VMEM((strips, ranks - 1, piece, BS), bf16),
+            dma((4 + strips,)),
+            dma((4 + strips,)),
+            dma((4 + strips,)),
+            dma((2,)),
+            dma((2,)),
+            dma((strips, ranks - 1)),
+            dma((strips, ranks - 1)),
+            pltpu.SemaphoreType.REGULAR,
+        ],
+        compiler_params=pltpu.CompilerParams(
+            collective_id=0, has_side_effects=True, vmem_limit_bytes=60 * 1024 * 1024
+        ),
+    )(part_rows, send_rows[0].T, col_index[0], basis.reshape(lb, BS, width), blocks[0])
+    return reduced[None]
+
+
 def solution(mesh):
     placed = (
         P(("grp", "mesh"), "col"),
@@ -67,6 +351,23 @@
         P(("grp", "mesh"), None, None),
         P(("grp", "mesh")),
     )
+    parts, cols, cores = mesh.shape["mesh"], mesh.shape["col"], mesh.shape["term"]
+
+    def local(basis, blocks, col_index, send_rows, part_rows):
+        lb = basis.shape[0] // BS
+        fits = (
+            cols == 2
+            and 2 <= parts <= 4
+            and cores == 2
+            and basis.shape[1] % BS == 0
+            and lb % cores == 0
+            and lb == 2 * blocks.shape[1]
+            and (2 * basis.shape[1]) % (2 * parts * 16) == 0
+        )
+        if fits:
+            return fused(parts, cores, basis, blocks, col_index, send_rows, part_rows)
+        return general(basis, blocks, col_index, send_rows, part_rows)
+
     return jax.shard_map(
         local,
         mesh=mesh,

time: 145 us -> 24.9 us (0.17)
  waiting for transfers between devices: 68.1 us -> 0 us
  matrix products: 24.9 us -> 0 us
  Pallas kernels: 0 us -> 22.6 us
  between operations: 18 us -> 0.66 us
  local copies, waits for them, and re-layouts: 15.3 us -> 1.57 us
  blocking collectives: 10.1 us -> 0 us
  starting transfers between devices: 6.23 us -> 0 us
    reduce_scatter x1 -> x0, waiting for transfers between devices: 64.5 us -> none  [local(): lax.psum_scatter(lax.dot_general(own_rows, rounded, (((0,), (0,)), ((), (...]
    dot_general x21 -> x0, matrix products: 24.9 us -> none  [the longest x20 23.7 us: accumulate(): jnp.einsum('bij,bjc->bic', term_blocks[:, k], picked, preferred_element_t...]
    pallas_call x0 -> x1, Pallas kernels: none -> 22.6 us  [fused(): pl.pallas_call(functools.partial(kernel, parts, cores), out_shape=jax.Sha...]
    gather x20 -> x0, local copies, waits for them, and re-layouts: 11.3 us -> none  [accumulate(): picked = jnp.take(extended, slot_index[:, k], axis=0)]
    all_gather x1 -> x0, blocking collectives: 10.1 us -> none  [local(): extended = lax.all_gather(ext_panel, 'col', axis=2, tiled=True)]
    ppermute x2 -> x0, starting transfers between devices: 6.22 us -> none  [from_behind(): return lax.ppermute(x, axis, pairs)]
    ppermute x2 -> x0, waiting for transfers between devices: 3.57 us -> none  [from_behind(): return lax.ppermute(x, axis, pairs)]
  transfers between devices with their start and end apart: 3 -> 0, of which waited for: 2 -> 0; matrix products, arithmetic and copies ran while one was open for 1% -> 0% of each run, Pallas kernels for 0% -> 0%
where the time goes in v2:
time: 24.9 us; the launch traced here: 24.8 us
  Pallas kernels  22.6 us (91%)
  local copies, waits for them, and re-layouts  1.57 us (6%)
  between operations  0.66 us (3%)
    pallas_call x1, Pallas kernels, fused(): pl.pallas_call(functools.partial(kernel, parts, cores), out_shape=jax.Sha...  22.6 us
    unnamed x1, local copies, waits for them, and re-layouts  1.57 us

profile of v2, /device:TPU:0, one launch (start us, length us, event | category | flops | bytes accessed | tf_op | source)
XLA Modules:
  0.0 24.8 jit_solution(6250084527681669548)
XLA Ops:
  0.7 22.6 %shard_map.55 = f32[64,512]{1,0:T(8,128)} custom-call(s32[1]{0:T(128)S(6)} %copy.7.part_hbm, s32[1,2]{1,0:T(1,128)} %bitcast.9, s32[2,20]{1,0:T(2,128)} %bitcast.8, bf16[4,128,256]{2,1,0:T(8,128)(2,1)} %bitcast.7, bf16[2,20,128,128]{3,2,1,0:T(8,128)(2,1)} %bitcast.5), custom_call_target="tpu_custom_call" | custom-call | tf_op jit(solution)/shard_map/pallas_call | solution.py:309
  23.2 1.6 %copy.8 = f32[1,64,512]{2,1,0:T(8,128)} copy(f32[1,64,512]{2,1,0:T(8,128)} %bitcast.6) | data formatting | bytes 262144

commit v3 on v2

--- a/solution.py
+++ b/solution.py
@@ -102,7 +102,8 @@
     c = lax.axis_index("col")
     t = lax.axis_index("term")
     strips, lb = basis_v.shape[:2]
-    width = strips * BS
+    lane = basis_v.shape[3]
+    width = strips * lane
     halo = send_ref.shape[0]
     rows, stored = blocks_v.shape[:2]
     ranks = 2 * parts
@@ -118,7 +119,7 @@
     everyone = range(strips)
 
     def strip(q):
-        return pl.ds(q * BS, BS)
+        return pl.ds(q * lane, lane)
 
     load_basis = [
         pltpu.make_async_copy(basis_ref.at[:, :, strip(q)], basis_v.at[q], local_sem.at[4 + q]) for q in everyone
@@ -187,7 +188,7 @@
             for i in range(lb):
                 ext[q, halo + i] = jnp.where(i < part_ref[0], raw[q, i], jnp.zeros((), jnp.bfloat16))
 
-    blank = jnp.zeros((strips, halo, BS, BS), jnp.bfloat16)
+    blank = jnp.zeros((strips, halo, BS, lane), jnp.bfloat16)
     for there, where in ((has_lower, low), (has_upper, high)):
 
         @pl.when(jnp.logical_not(there))
@@ -212,8 +213,8 @@
 
     def turn(ext, where):
         for q in everyone:
-            body = ext[q, pl.ds(halo, lb)].reshape(lb * BS, BS)
-            turned[pl.ds(where * width + q * BS, BS)] = body.T
+            body = ext[q, pl.ds(halo, lb)].reshape(lb * BS, lane)
+            turned[pl.ds(where * width + q * lane, lane)] = body.T
 
     def share(d, q):
         to, r = peer(d)
@@ -240,7 +241,7 @@
     for r in range(rows):
         value = product(ext_own, r)
         for q in everyone:
-            p_send[q, pl.ds(r * BS, BS)] = value[:, q * BS : (q + 1) * BS]
+            p_send[q, pl.ds(r * BS, BS)] = value[:, q * lane : (q + 1) * lane]
     for q in everyone:
         swap[q].start()
     across.wait_recv()
@@ -259,7 +260,7 @@
     for r in range(rows):
         value = product(ext_other, r)
         for q in everyone:
-            p_all[q, pl.ds(c * rows * BS + r * BS, BS)] = value[:, q * BS : (q + 1) * BS]
+            p_all[q, pl.ds(c * rows * BS + r * BS, BS)] = value[:, q * lane : (q + 1) * lane]
     pl.semaphore_wait(ok_sem, sides)
 
     for q in everyone:
@@ -279,8 +280,8 @@
                 crossed = crossed + g_recv[q, d - 1].astype(jnp.float32)
             else:
                 same = same + g_recv[q, d - 1].astype(jnp.float32)
-        out_ref[:, pl.ds(pl.multiple_of((1 - c) * width + q * BS, BS), BS)] = same
-        out_ref[:, pl.ds(pl.multiple_of(c * width + q * BS, BS), BS)] = crossed
+        out_ref[:, pl.ds(pl.multiple_of((1 - c) * width + q * lane, lane), lane)] = same
+        out_ref[:, pl.ds(pl.multiple_of(c * width + q * lane, lane), lane)] = crossed
 
     across.wait_send()
     inner.wait_send()
@@ -300,7 +301,8 @@
     halo = send_rows.shape[2]
     rows, stored = blocks.shape[1:3]
     full = 2 * width
-    strips = width // BS
+    strips = 1
+    lane = width // strips
     ranks = 2 * parts
     piece = full // ranks
     bf16 = jnp.bfloat16
@@ -315,18 +317,18 @@
             pltpu.SMEM((1,), jnp.int32),
             pltpu.SMEM((halo, 2), jnp.int32),
             pltpu.SMEM((rows, stored), jnp.int32),
-            pltpu.VMEM((strips, lb, BS, BS), bf16),
+            pltpu.VMEM((strips, lb, BS, lane), bf16),
             pltpu.VMEM((rows, stored, BS, BS), bf16),
-            pltpu.VMEM((strips, lb, BS, BS), bf16),
-            pltpu.VMEM((strips, lb + 2 * halo, BS, BS), bf16),
-            pltpu.VMEM((strips, lb + 2 * halo, BS, BS), bf16),
-            pltpu.VMEM((2, strips, halo, BS, BS), bf16),
+            pltpu.VMEM((strips, lb, BS, lane), bf16),
+            pltpu.VMEM((strips, lb + 2 * halo, BS, lane), bf16),
+            pltpu.VMEM((strips, lb + 2 * halo, BS, lane), bf16),
+            pltpu.VMEM((2, strips, halo, BS, lane), bf16),
             pltpu.VMEM((full, lb * BS), bf16),
-            pltpu.VMEM((strips, rows * BS, BS), bf16),
-            pltpu.VMEM((strips, lb * BS, BS), bf16),
-            pltpu.VMEM((strips, full, BS), jnp.float32),
-            pltpu.VMEM((strips, full, BS), bf16),
-            pltpu.VMEM((strips, ranks - 1, piece, BS), bf16),
+            pltpu.VMEM((strips, rows * BS, lane), bf16),
+            pltpu.VMEM((strips, lb * BS, lane), bf16),
+            pltpu.VMEM((strips, full, lane), jnp.float32),
+            pltpu.VMEM((strips, full, lane), bf16),
+            pltpu.VMEM((strips, ranks - 1, piece, lane), bf16),
             dma((4 + strips,)),
             dma((4 + strips,)),
             dma((4 + strips,)),

time: 24.9 us -> 24.2 us (0.972)
  Pallas kernels: 22.6 us -> 21.8 us
    pallas_call x1, Pallas kernels: 22.6 us -> 21.8 us  [fused(): pl.pallas_call(functools.partial(kernel, parts, cores), out_shape=jax.Sha...]
where the time goes in v3:
time: 24.2 us; the launch traced here: 24.1 us
  Pallas kernels  21.8 us (90%)
  local copies, waits for them, and re-layouts  1.57 us (6%)
  between operations  0.66 us (3%)
    pallas_call x1, Pallas kernels, fused(): pl.pallas_call(functools.partial(kernel, parts, cores), out_shape=jax.Sha...  21.8 us
    unnamed x1, local copies, waits for them, and re-layouts  1.57 us

profile of v3, /device:TPU:0, one launch (start us, length us, event | category | flops | bytes accessed | tf_op | source)
XLA Modules:
  0.0 24.1 jit_solution(2077103649442041700)
XLA Ops:
  0.7 21.8 %shard_map.55 = f32[64,512]{1,0:T(8,128)} custom-call(s32[1]{0:T(128)S(6)} %copy.7.part_hbm, s32[1,2]{1,0:T(1,128)} %bitcast.9, s32[2,20]{1,0:T(2,128)} %bitcast.8, bf16[4,128,256]{2,1,0:T(8,128)(2,1)} %bitcast.7, bf16[2,20,128,128]{3,2,1,0:T(8,128)(2,1)} %bitcast.5), custom_call_target="tpu_custom_call" | custom-call | tf_op jit(solution)/shard_map/pallas_call | solution.py:311
  22.5 1.6 %copy.8 = f32[1,64,512]{2,1,0:T(8,128)} copy(f32[1,64,512]{2,1,0:T(8,128)} %bitcast.6) | data formatting | bytes 262144
